TPU v7x, 32 devices: a whole 2x2x4 slice. The times are simulated.
32 devices in a mesh: parts: 2 (over x), seq: 16 (over z, y, core).
Axes of the slice: x: 2, y: 2, z: 4, core: 2. Of those that a mesh axis runs over, the one named last changes fastest.
Arguments:
- queries: bfloat16 [4096, 1024], P(('parts', 'seq')), parts along dimension 0, may hold values from -6 to 6
- keys: bfloat16 [4096, 1024], P(('parts', 'seq')), parts along dimension 0, may hold values from -6 to 6
- values: bfloat16 [4096, 1024], P(('parts', 'seq')), parts along dimension 0, may hold values from -6 to 6
- log_forget: float32 [8, 4096], P(None, ('parts', 'seq')), parts along dimension 1, may hold values from -5 to 0
- input_gate: float32 [8, 4096], P(None, ('parts', 'seq')), parts along dimension 1, may hold values from 0.1 to 1
- ridge: float32 [8], replicated, may hold values from 0.25 to 4
- gain: float32 [1024], replicated, may hold values from 0.25 to 1.75
- out_weight: bfloat16 [1024, 2048], P('seq'), may hold values from -0.1875 to 0.1875
Outputs:
- mixed: bfloat16 [4096, 2048], P(('parts', 'seq')), parts along dimension 0
There are 2 independent parts, one for each index of `parts`. A program takes and returns all parts, laid end to end along the dimension named above; an argument that names none is the same for every part. Nothing has to cross between parts.
All inputs are finite; a program needn't handle non-finite values. Where the computation divides by a largest or mean magnitude, that divisor is 1e-20 or more.
Results may differ from a plain program's by a relative error of at most 0.007.
Values may be sent and summed in bfloat16 or wider, within the bound.
A program may use at most 192 MiB of HBM per device.

v0:
```python
import jax
import jax.numpy as jnp
from jax import lax
from jax.sharding import PartitionSpec as P

HEADS = 8
DH = 128
C = 128
NEWTON = 6
CORR = 4


highest = lax.Precision.HIGHEST


def carried_in(array, axis, join, neutral):
    place = lax.axis_index(axis)
    gathered = jax.tree.map(
        lambda a, kind: lax.all_gather(a.astype(kind), axis), array, (jnp.bfloat16, jnp.bfloat16)
    )
    state = jax.tree.map(lambda a, e: jnp.zeros_like(a) + jnp.asarray(e, a.dtype), array, neutral)

    def one(step, state):
        return join(
            state,
            jax.tree.map(
                lambda a, own: lax.dynamic_index_in_dim(a, step, 0, False).astype(own.dtype),
                gathered,
                array,
            ),
        )

    return lax.fori_loop(0, place, one, state)


def prefix(value, axis, join, neutral):
    count, mine = (lax.axis_size(axis), lax.axis_index(axis))
    pieces = jax.tree.map(lambda part: lax.all_gather(part, axis), value)
    total = jax.tree.map(
        lambda part, zero: jnp.full_like(part, 0) + jnp.asarray(zero, part.dtype), value, neutral
    )

    def step(position, total):
        longer = join(total, jax.tree.map(lambda part: part[position], pieces))
        return jax.tree.map(lambda new, old: jnp.where(position < mine, new, old), longer, total)

    return lax.fori_loop(0, count - 1, step, total)


def product(left, right):
    return jnp.matmul(left, right, precision=highest)


def unit_rows(field):
    return field * lax.rsqrt(jnp.sum(field * field, axis=-1, keepdims=True) + 1e-06)


def add_pairs(earlier, later):
    shrink = jnp.exp(later[0])[:, None, None]
    return (earlier[0] + later[0], shrink * earlier[1] + later[1])


def newton_inverse(system):
    bound = jnp.max(jnp.sum(jnp.abs(system), axis=-1), axis=-1)
    identity = jnp.eye(system.shape[-1], dtype=system.dtype)
    approx = identity / bound[..., None, None]
    for iteration in range(NEWTON):
        approx = product(approx, 2.0 * identity - product(system, approx))
    return approx


def solve_blocks(query_rows, key_t, beta_keys, start_gram, pre_gram, decay_row, mixing, ridge_col):
    identity = jnp.eye(query_rows.shape[-1], dtype=query_rows.dtype)
    system = start_gram + pre_gram + ridge_col * identity
    inverse = newton_inverse(system)
    solved = product(query_rows, inverse)
    for iteration in range(CORR - 1):
        attention_scores = mixing * product(solved, key_t)
        applied = (
            decay_row * product(solved, start_gram)
            + product(attention_scores, beta_keys)
            + ridge_col * solved
        )
        solved = solved + product(query_rows - applied, inverse)
    attention_scores = mixing * product(solved, key_t)
    return (solved, attention_scores)


def shift_down(field):
    return jnp.concatenate([jnp.zeros_like(field), field[:-1]], axis=0)


def on_device(queries, keys, values, log_forget, input_gate, ridge, gain, out_weight):
    tokens = queries.shape[0]
    count = tokens // C

    def blocks(field):
        return field.astype(jnp.float32).reshape(count, C, HEADS, DH).transpose(0, 2, 1, 3)

    def gate_blocks(field):
        return field.reshape(HEADS, count, C).transpose(1, 0, 2)

    query_all = unit_rows(blocks(queries))
    key_all = unit_rows(blocks(keys))
    value_all = blocks(values)
    forget_all = gate_blocks(log_forget)
    beta_all = gate_blocks(input_gate)
    running = jnp.cumsum(forget_all, axis=-1)
    block_decay = running[..., -1]
    decay_row = jnp.exp(running)[..., None]
    lower_mask = jnp.tril(jnp.ones((C, C), jnp.float32))
    mixing = lower_mask * jnp.exp(jnp.minimum(running[..., :, None] - running[..., None, :], 0.0))
    tail = (jnp.exp(block_decay[..., None] - running) * beta_all)[..., None]
    beta_col = beta_all[..., None]
    beta_keys = beta_col * key_all
    beta_values = beta_col * value_all
    key_t = jnp.swapaxes(key_all, -1, -2)
    block_grams = product(key_t, tail * key_all)
    block_states = product(key_t, tail * value_all)
    pre_grams = product(key_t, beta_keys)
    level_incl = jnp.cumsum(block_decay, axis=0)
    level_exclusive = level_incl - block_decay
    block_mask = jnp.tril(jnp.ones((count, count), jnp.float32))
    carry_weights = block_mask[:, :, None] * jnp.exp(
        jnp.minimum(level_incl[:, None, :] - level_incl[None, :, :], 0.0)
    )
    gram_incl = jnp.einsum("bch,chij->bhij", carry_weights, block_grams, precision=highest)
    state_incl = jnp.einsum("bch,chij->bhij", carry_weights, block_states, precision=highest)
    gram_local = shift_down(gram_incl)
    state_local = shift_down(state_incl)
    section_decay = level_incl[-1]
    gram_total = gram_incl[-1]
    state_total = state_incl[-1]
    carried = jnp.exp(level_exclusive)[..., None, None]
    ridge_col = ridge[None, :, None, None]
    zeros = jnp.zeros((HEADS, DH, DH), jnp.float32)
    zero_levels = jnp.zeros((HEADS,), jnp.float32)
    decay_before, gram_before = carried_in(
        (section_decay, gram_total), "seq", add_pairs, (zero_levels, zeros)
    )
    start_gram = carried * gram_before[None] + gram_local
    solved, attention_scores = solve_blocks(
        query_all, key_t, beta_keys, start_gram, pre_grams, decay_row, mixing, ridge_col
    )
    decay_again, state_before = prefix(
        (section_decay, state_total), "seq", add_pairs, (zero_levels, zeros)
    )
    start_state = carried * state_before[None] + state_local
    outputs = decay_row * product(solved, start_state) + product(attention_scores, beta_values)
    normed = outputs * lax.rsqrt(jnp.mean(outputs * outputs, axis=-1, keepdims=True) + 1e-06)
    normed = normed.transpose(0, 2, 1, 3).reshape(tokens, HEADS * DH) * gain
    normed = normed.astype(jnp.bfloat16)
    mixed = jnp.dot(
        normed,
        lax.all_gather(out_weight, "seq", axis=0, tiled=True),
        preferred_element_type=jnp.float32,
    )
    return mixed.astype(jnp.bfloat16)


def solution(mesh):
    placed = (
        P(("parts", "seq"), None),
        P(("parts", "seq"), None),
        P(("parts", "seq"), None),
        P(None, ("parts", "seq")),
        P(None, ("parts", "seq")),
        P(),
        P(),
        P("seq", None),
    )
    return jax.shard_map(
        on_device, mesh=mesh, in_specs=placed, out_specs=P(("parts", "seq"), None), check_vma=False
    )
```

profile of v0, /device:TPU:0, one launch (start us, length us, event | category | flops | bytes accessed | tf_op | source)
XLA Modules:
  0.0 203.0 jit_solution(14111731885373058151)
XLA Ops:
  6.5 1.1 copy.277
  7.7 1.1 copy.189
  8.9 1.0 reduce_window_sum.19
  10.0 0.8 bitcast_exponential_fusion
  10.8 1.9 fusion.14
  12.8 0.1 copy.276
  12.9 2.0 convolution_multiply_fusion.2
  15.0 0.7 all-gather.8.cloned.1.call-update
  15.7 23.0 %all-gather.1 = f32[16,8,1]{1,2,0:T(1,128)S(1)} all-gather(f32[1,8,1]{1,2,0:T(1,128)S(1)} %copy.278), channel_id=3, replica_groups=mesh['parts'=2,'seq'=16] {'seq'}, dimensions={0}, use_global_device_ids=true | all-gather | bytes 544 | tf_op jit(solution)/shard_map/all_gather | solution.py:38
  38.7 17.4 %all-gather.3 = bf16[16,8,1]{1,2,0:T(2,128)(2,1)S(1)} all-gather(bf16[1,8,1]{1,2,0:T(2,128)(2,1)S(1)} %convert_element_type.59), channel_id=5, replica_groups=mesh['parts'=2,'seq'=16] {'seq'}, dimensions={0}, use_global_device_ids=true | all-gather | bytes 272 | tf_op jit(solution)/shard_map/all_gather | solution.py:19
  56.4 9.7 %all-gather.10.cloned.1.call-done = bf16[128,128,128]{2,1,0:T(8,128)(2,1)} async-done(((bf16[8,128,128]{2,1,0:T(8,128)(2,1)}), bf16[128,128,128]{2,1,0:T(8,128)(2,1)}) %all-gather.10.cloned.1.call-update) | async-done | bytes 4194320 | tf_op jit(solution)/shard_map/all_gather | solution.py:19
  66.2 0.2 while.26
  66.4 0.2 copy.196
  66.6 1.2 abs_reduce_fusion
  68.0 1.3 convolution_subtract_fusion.5
  69.3 1.1 fusion.37
  70.4 1.1 convolution_subtract_fusion.4
  71.5 0.7 fusion.82
  72.1 1.1 convolution_subtract_fusion.3
  73.2 0.6 fusion.83
  73.8 1.1 convolution_subtract_fusion.2
  74.9 0.6 fusion.84
  75.5 1.1 convolution_subtract_fusion.1
  76.6 0.6 fusion.85
  77.3 1.1 convolution_subtract_fusion
  78.3 0.6 fusion.86
  79.0 1.2 fusion.30
  80.2 1.0 copy.214
  81.2 1.3 convolution_multiply_fusion.8
  82.5 0.7 convolution_multiply_fusion.7
  83.2 2.2 %fusion.9 = f32[8,128,128]{1,2,0:T(8,128)S(1)} fusion(f32[8,128,128]{1,2,0:T(8,128)S(1)} %convolution_multiply_fusion.8, f32[8,128,128]{2,1,0:T(8,128)S(1)} %convolution_multiply_fusion.7, f32[8,128,128]{1,2,0:T(8,128)} %copy.214, f32[1,8,128,128]{2,3,1,0:T(8,128)S(1)} %bitcast.176, f32[1,8,128,128]{2,3,1,0:T(8,128)S(1)} %bitcast.168, f32[8]{0:T(128)S(1)} %copy-done.5, ...), kind=kOutput, calls=%fused_computation.38 | convolution fusion | flops 202244096 | bytes 3158048 | tf_op jit(solution)/shard_map/dot_general | solution.py:51
  85.5 1.0 convolution_add_fusion.5
  86.5 1.1 convolution_multiply_fusion.5
  87.6 0.6 convolution_multiply_fusion.6
  88.2 1.2 fusion.11
  89.4 1.0 convolution_add_fusion.3
  90.5 0.6 convolution_multiply_fusion.4
  91.1 1.1 convolution_multiply_fusion.3
  92.2 1.2 fusion.13
  93.4 1.0 convolution_add_fusion.1
  94.4 1.3 convolution_multiply_fusion
  95.8 46.0 %all-gather.12.cloned.1.call-done = f32[128,128,128]{2,1,0:T(8,128)} async-done(((f32[8,128,128]{2,1,0:T(8,128)}), f32[128,128,128]{2,1,0:T(8,128)}) %all-gather.12.cloned.1.call-update) | async-done | bytes 8388624 | tf_op jit(solution)/shard_map/all_gather | solution.py:38
  141.8 18.3 %while.27 = (s32[]{:T(128)}, f32[8,128,128]{2,1,0:T(8,128)S(1)}, s32[]{:T(128)}, f32[16,8]{1,0:T(8,128)S(1)}, f32[16,8,128,128]{3,2,1,0:T(8,128)}, /*index=5*/s32[]{:T(128)}, s32[]{:T(128)}) while((s32[]{:T(128)}, f32[8,128,128]{2,1,0:T(8,128)S(1)}, s32[]{:T(128)}, f32[16,8]{1,0:T(8,128)S(1)}, f32[16,8,128,128]{3,2,1,0:T(8,128)}, ...), condition=%wide.region_8.9_spmd.clone, body=%wide.region_7.8_spmd.clone.sunk | while | flops 524292 | bytes 1573065 | solution.py:47
  141.8 1.2 fusion.131
  143.0 1.2 fusion.131
  144.3 1.2 fusion.131
  145.5 1.2 fusion.131
  146.7 1.2 fusion.131
  147.9 1.2 fusion.131
  149.1 1.2 fusion.131
  150.4 1.2 fusion.131
  151.6 1.2 fusion.131
  152.8 1.2 fusion.131
  154.0 1.2 fusion.131
  155.3 1.2 fusion.131
  156.5 1.2 fusion.131
  157.7 1.2 fusion.131
  158.9 1.2 fusion.131
  160.1 0.2 copy.236
  160.3 0.6 convolution_multiply_fusion.1
  161.0 1.2 multiply_reduce_fusion
  162.3 0.2 fusion.15
  162.5 30.3 %all-gather.8.cloned.1.call-done = bf16[1024,2048]{1,0:T(8,128)(2,1)} async-done(((bf16[64,2048]{1,0:T(8,128)(2,1)}), bf16[1024,2048]{1,0:T(8,128)(2,1)}) %all-gather.8.cloned.1.call-update) | async-done | bytes 4194320 | tf_op jit(solution)/shard_map/all_gather | solution.py:155
  192.8 3.7 %convolution_convert_fusion = bf16[128,2048]{1,0:T(8,128)(2,1)} fusion(bf16[128,1024]{0,1:T(8,128)(2,1)S(1)} %fusion.15, bf16[1024,2048]{1,0:T(8,128)(2,1)} %all-gather.8.cloned.1.call-done), kind=kOutput, calls=%fused_computation.5 | convolution fusion | flops 537133056 | bytes 4980736 | tf_op jit(solution)/shard_map/dot_general | solution.py:153
  (52 shorter events, 1.0 us)
Async XLA Ops:
  6.5 6.2 %copy-start.3 = (bf16[128,1024]{1,0:T(8,128)(2,1)S(1)}, bf16[128,1024]{1,0:T(8,128)(2,1)}, u32[]{:S(2)}) copy-start(bf16[128,1024]{1,0:T(8,128)(2,1)} %param.14) | copy-start | bytes 786436
  6.5 59.6 %all-gather.10.cloned.1.call-start = ((), (), s32[]{:S(2)}) async-start(), calls=%async_computation.1 | async-start | bytes 4456448 | tf_op jit(solution)/shard_map/all_gather | solution.py:19
  12.7 129.0 %all-gather.12.cloned.1.call-start = ((), (), s32[]{:S(2)}) async-start(), calls=%async_computation.2 | async-start | bytes 8912896 | tf_op jit(solution)/shard_map/all_gather | solution.py:38
  12.9 53.3 %copy-start = (f32[128,1024]{0,1:T(8,128)}, f32[128,1024]{0,1:T(8,128)S(1)}, u32[]{:S(2)}) copy-start(f32[128,1024]{0,1:T(8,128)S(1)} %copy.276) | copy-start | bytes 1572868
  14.9 177.8 %all-gather.8.cloned.1.call-start = ((), (), s32[]{:S(2)}) async-start(), calls=%async_computation | async-start | bytes 4456448 | tf_op jit(solution)/shard_map/all_gather | solution.py:155
  56.4 10.2 %copy-start.4 = (f32[8,128]{1,0:T(8,128)S(1)}, f32[8,128]{1,0:T(8,128)}, u32[]{:S(2)}) copy-start(f32[8,128]{1,0:T(8,128)} %param.16) | copy-start | bytes 12292
  56.4 10.2 %copy-start.5 = (f32[8]{0:T(128)S(1)}, f32[8]{0:T(128)}, u32[]{:S(2)}) copy-start(f32[8]{0:T(128)} %param.17) | copy-start | bytes 100
  81.2 4.2 %copy-start.2 = (f32[8,128,128]{1,2,0:T(8,128)S(1)}, f32[8,128,128]{1,2,0:T(8,128)}, u32[]{:S(2)}) copy-start(f32[8,128,128]{1,2,0:T(8,128)} %copy.214) | copy-start | bytes 1572868
  141.8 19.2 %copy-start.1 = (f32[128,1024]{0,1:T(8,128)S(1)}, f32[128,1024]{0,1:T(8,128)}, u32[]{:S(2)}) copy-start(f32[128,1024]{0,1:T(8,128)} %copy-done) | copy-start | bytes 1572868
  160.1 2.2 %copy-start.6 = (f32[1024]{0:T(1024)S(1)}, f32[1024]{0:T(1024)}, u32[]{:S(2)}) copy-start(f32[1024]{0:T(1024)} %param.18) | copy-start | bytes 12292
Sparse Core Ops, SparseCore 0:
  12.8 53.2 all-gather.9
  68.3 73.3 all-gather.11
  143.9 48.8 all-gather.7
where the time goes:
time: 204 us; the launch traced here: 203 us
  waiting for transfers between devices  86.7 us (42%)
  blocking collectives  40.4 us (20%)
  matrix products  37.4 us (18%)
  other arithmetic  20 us (10%)
  between operations  13.5 us (7%)
  local copies, waits for them, and re-layouts  4.3 us (2%)
    all_gather x1, waiting for transfers between devices, prefix(): pieces = jax.tree.map(lambda part: lax.all_gather(part, axis), value)  46 us
    dot_general x31, matrix products, product(): return jnp.matmul(left, right, precision=highest)  33.7 us
    all_gather x1, waiting for transfers between devices, on_device(): lax.all_gather(out_weight, 'seq', axis=0, tiled=True)  30.3 us
    all_gather x1, blocking collectives, prefix(): pieces = jax.tree.map(lambda part: lax.all_gather(part, axis), value)  23 us
    select_n x15, other arithmetic, step(): jnp.where(position < mine, new, old)  17.7 us
    all_gather x1, blocking collectives, carried_in(): lax.all_gather(a.astype(kind), axis)  17.4 us
    all_gather x1, waiting for transfers between devices, carried_in(): lax.all_gather(a.astype(kind), axis)  9.74 us
  transfers between devices with their start and end apart: 3, of which 3 were waited for; matrix products, arithmetic and copies ran while one was open for 26% of the time, Pallas kernels for 0%

commit v1 on v0

v1 whole, which is shorter than its diff:
```python
import functools

import jax
import jax.numpy as jnp
from jax import lax
from jax.experimental import pallas as pl
from jax.experimental.pallas import tpu as pltpu
from jax.sharding import PartitionSpec as P

NEWTON = 6
CORR = 4
EPS = 1e-06
F32 = jnp.float32
BF16 = jnp.bfloat16
MESH = pl.DeviceIdType.MESH
HIGHEST = lax.Precision.HIGHEST


def dot(a, b, dims=((1,), (0,)), precision=None):
    return lax.dot_general(a, b, (dims, ((), ())), precision=precision, preferred_element_type=F32)


def low(a):
    return a.astype(BF16)


def split_dot(a, b):
    high = low(a)
    return dot(high, b) + dot(low(a - high.astype(F32)), b)


def kernel(
    layers, ring, heads, q_ref, k_ref, v_ref, forget_ref, gate_ref, ridge_ref, gain_ref, w_ref,
    out_ref, level, gram_out, gram_in, gram_chain_in, gram_chain_out, gram_back, gram_full,
    state_out, state_in, state_chain_in, state_chain_out, state_back, state_full,
    weights, y_ref,
    level_sems, piece_sems, chain_sems, back_sems, z_sems, y_sems, core_sems,
):
    me = lax.axis_index("seq")
    layer, rank = me // ring, me % ring
    share = heads // ring
    tokens = q_ref.shape[0]
    dh = q_ref.shape[1] // heads
    rows = w_ref.shape[0]
    pending = []

    def others():
        return [(rank + d) % ring for d in range(1, ring)]

    def send(src, dst, sems, slot_out, slot_in, target):
        copy = pltpu.make_async_remote_copy(
            src_ref=src, dst_ref=dst, send_sem=sems[0].at[slot_out], recv_sem=sems[1].at[slot_in],
            device_id={"seq": target}, device_id_type=MESH,
        )
        copy.start()
        return copy

    def arrived(dst, sems, slot):
        pltpu.make_async_remote_copy(
            src_ref=dst, dst_ref=dst, send_sem=sems[0].at[slot], recv_sem=sems[1].at[slot],
            device_id={"seq": (me + 1) % (layers * ring)}, device_id_type=MESH,
        ).wait_recv()

    def shard(index):
        return weights.at[pl.ds(pl.multiple_of(index * rows, rows), rows)]

    barrier = pltpu.get_barrier_semaphore()
    partners = [layer * ring + p for p in others()]
    partners += [((layer + d) % layers) * ring + rank for d in range(1, layers)]
    for partner in partners:
        pl.semaphore_signal(barrier, inc=1, device_id={"seq": partner}, device_id_type=MESH)
    pl.semaphore_wait(barrier, len(partners))

    row_id = lax.broadcasted_iota(jnp.int32, (tokens, tokens), 0)
    col_id = lax.broadcasted_iota(jnp.int32, (tokens, tokens), 1)
    upper = (row_id <= col_id).astype(F32)
    lower = row_id >= col_id
    eye = (row_id == col_id).astype(F32)
    forget = forget_ref[...]
    run_row = dot(forget, upper, precision=HIGHEST)
    run_col = dot(lower.astype(F32), forget, ((1,), (1,)), precision=HIGHEST)
    gate_col = dot(eye, gate_ref[...], ((1,), (1,)), precision=HIGHEST)
    last = jnp.sum(forget, axis=1, keepdims=True)
    level[rank] = jnp.broadcast_to(last, (heads, dh))
    for p in others():
        pending.append(send(level.at[rank], level.at[rank], level_sems, p, rank, layer * ring + p))

    across = (rank + ring // 2) % ring
    sibling = rank + 1 - 2 * (rank % 2)
    pending.append(send(w_ref, shard(me), y_sems, layer, layer, layer * ring + across))
    pending.append(send(w_ref, shard(me), core_sems, layer * 2, layer * 2 + rank // 2, layer * ring + sibling))

    def to_column():
        for d in range(1, layers):
            there = (layer + d) % layers
            pending.append(send(w_ref, shard(me), z_sems, there, layer, there * ring + rank))

    def from_column(d):
        there = (layer + d) % layers
        piece = shard(there * ring + rank)
        arrived(piece, z_sems, there)
        pending.append(send(piece, piece, y_sems, there, there, layer * ring + across))
        pending.append(send(piece, piece, core_sems, there * 2, there * 2 + rank // 2, layer * ring + sibling))

    def from_across(d):
        there = (layer + d) % layers
        piece = shard(there * ring + across)
        arrived(piece, y_sems, there)
        pending.append(send(piece, piece, core_sems, there * 2 + 1, there * 2 + across // 2, layer * ring + sibling))

    pre, keys_t, keys_low, beta_keys = [], [], [], []
    mixes, decays = [], []
    for h in range(heads):
        lanes = slice(h * dh, (h + 1) * dh)
        raw = k_ref[:, lanes]
        key = raw.astype(F32)
        scale = lax.rsqrt(jnp.sum(key * key, axis=1, keepdims=True) + EPS)
        beta = gate_col[:, h:h + 1]
        run = run_col[:, h:h + 1]
        tail = jnp.exp(last[h:h + 1, :] - run) * beta
        value = v_ref[:, lanes].astype(F32)
        unit = scale * key
        right = jnp.concatenate(
            [low((tail * scale) * unit), low((beta * scale) * unit), low((tail * scale) * value),
             low(scale * eye)], axis=1)
        made = dot(raw, right, ((0,), (0,)))
        gram_out[h] = low(made[:, :dh])
        pre.append(made[:, dh:2 * dh])
        state_out[h] = made[:, 2 * dh:3 * dh]
        keys_t.append(low(made[:, 3 * dh:]))
        beta_keys.append(low(beta * unit))
        mixes.append(jnp.where(lower, jnp.exp(jnp.minimum(run - run_row[h:h + 1, :], 0.0)), 0.0))
        decays.append(jnp.exp(run))

    mine = pl.ds(rank * share, share)
    kinds = (
        (gram_out, gram_in, gram_chain_in, gram_chain_out, gram_back, gram_full, 0),
        (state_out, state_in, state_chain_in, state_chain_out, state_back, state_full, 1),
    )

    def sems_of(sems, kind):
        return (sems[0].at[kind], sems[1].at[kind])

    for outgoing, incoming, *_, kind in kinds:
        for p in others():
            pending.append(send(
                outgoing.at[pl.ds(p * share, share)], incoming.at[rank],
                sems_of(piece_sems, kind), p, rank, layer * ring + p))
        incoming[rank] = outgoing[mine]
    to_column()

    for p in others():
        arrived(level.at[p], level_sems, p)
    chained = []

    def scan(outgoing, incoming, chain_in, chain_out, back, full, kind):
        for p in others():
            arrived(incoming.at[p], sems_of(piece_sems, kind), p)
        kept = incoming.dtype
        shrink, total = [], []
        for j in range(share):
            steps = [jnp.exp(level[p, pl.ds(rank * share + j, 1), :]) for p in range(ring)]
            whole = jnp.zeros((dh, dh), F32)
            for p in range(ring):
                whole = steps[p] * whole + incoming[p, j].astype(F32)
            shrink.append(steps)
            total.append(whole)

        @pl.when(layer == 0)
        def _():
            chain_in[...] = jnp.zeros_like(chain_in)

        for j in range(share):
            @pl.when(layer > 0)
            def _():
                arrived(chain_in.at[j], sems_of(chain_sems, kind), j)

            @pl.when(layer < layers - 1)
            def _():
                steps = shrink[j]
                over = steps[0]
                for p in range(1, ring):
                    over = over * steps[p]
                chain_out[j] = (over * chain_in[j].astype(F32) + total[j]).astype(kept)
                send(chain_out.at[j], chain_in.at[j], sems_of(chain_sems, kind), j, j, me + ring)
        for j in range(share):
            current = chain_in[j].astype(F32)
            for p in range(ring):
                back[p, j] = current.astype(kept)
                if p < ring - 1:
                    current = shrink[j][p] * current + incoming[p, j].astype(F32)
        for p in others():
            pending.append(send(back.at[p], full.at[mine], sems_of(back_sems, kind), p, rank, layer * ring + p))
        full[mine] = back[rank]
        chained.append((chain_out, chain_in, kind))

    scan(*kinds[0])
    scan(*kinds[1])
    for p in others():
        arrived(gram_full.at[pl.ds(p * share, share)], sems_of(back_sems, 0), p)
    ahead = list(range(1, layers))
    if ahead:
        from_column(ahead.pop(0))

    starts = [gram_full[h] for h in range(heads)]
    systems, inverses, bounds = [], [], []
    for h in range(heads):
        system = starts[h].astype(F32) + pre[h] + ridge_ref[h] * eye
        bound = jnp.max(jnp.sum(jnp.abs(system), axis=0, keepdims=True), axis=1, keepdims=True)
        inv = 1.0 / bound
        inverses.append(low((2.0 * eye - system * inv) * inv))
        systems.append(low(system))
    for step in range(NEWTON - 1):
        rests = [low(2.0 * eye - dot(systems[h], inverses[h])) for h in range(heads)]
        inverses = [low(dot(inverses[h], rests[h])) for h in range(heads)]
    from_across(0)
    if ahead:
        from_column(ahead.pop(0))

    both = [jnp.concatenate([starts[h], keys_t[h]], axis=1) for h in range(heads)]
    queries, solved = [], []
    for h in range(heads):
        query = q_ref[:, h * dh:(h + 1) * dh].astype(F32)
        query = query * lax.rsqrt(jnp.sum(query * query, axis=1, keepdims=True) + EPS)
        queries.append(query)
        solved.append(dot(low(query), inverses[h]))
    done = 1
    for step in range(CORR - 1):
        for h in range(heads):
            joint = dot(low(solved[h]), both[h])
            applied = (
                decays[h] * joint[:, :dh]
                + dot(low(mixes[h] * joint[:, dh:]), beta_keys[h])
                + ridge_ref[h] * solved[h]
            )
            solved[h] = solved[h] + dot(low(queries[h] - applied), inverses[h])
        while ahead and (step == CORR - 2 or len(ahead) > CORR - 2 - step):
            from_column(ahead.pop(0))
        if done < layers:
            from_across(done)
            done += 1
    while done < layers:
        from_across(done)
        done += 1

    for p in others():
        arrived(state_full.at[pl.ds(p * share, share)], sems_of(back_sems, 1), p)
    for h in range(heads):
        lanes = slice(h * dh, (h + 1) * dh)
        scores = mixes[h] * split_dot(solved[h], keys_t[h])
        value = low(gate_col[:, h:h + 1] * v_ref[:, lanes].astype(F32))
        state = state_full[h]
        output = decays[h] * split_dot(solved[h], low(state)) + dot(low(scores), value)
        output = output + decays[h] * dot(low(solved[h]), low(state - low(state).astype(F32)))
        norm = lax.rsqrt(jnp.mean(output * output, axis=1, keepdims=True) + EPS)
        y_ref[:, lanes] = low(output * norm * gain_ref[:, lanes])

    weights[pl.ds(pl.multiple_of(me * rows, rows), rows), :] = w_ref[...]
    other = sibling
    for there in range(layers):
        for half in range(ring // 2):
            arrived(shard(there * ring + half * 2 + other % 2), core_sems, there * 2 + half)
    columns = w_ref.shape[1]
    width = min(512, columns)
    for c in range(0, columns, width):
        out_ref[:, c:c + width] = low(dot(y_ref[...], weights[:, c:c + width]))

    for copy in pending:
        copy.wait_send()
    for chain_out, chain_in, kind in chained:
        @pl.when(layer < layers - 1)
        def _():
            for j in range(share):
                sems = sems_of(chain_sems, kind)
                pltpu.make_async_remote_copy(
                    src_ref=chain_out.at[j], dst_ref=chain_in.at[j], send_sem=sems[0].at[j],
                    recv_sem=sems[1].at[j], device_id={"seq": me + ring}, device_id_type=MESH,
                ).wait_send()


def wrapped(body, *refs):
    tail = refs[-14:]
    pairs = [(tail[i], tail[i + 1]) for i in range(0, 14, 2)]
    body(*refs[:-14], *pairs)


def solution(mesh):
    n = mesh.shape["seq"]
    ring = 4
    layers = n // ring

    def on_device(queries, keys, values, log_forget, input_gate, ridge, gain, out_weight):
        tokens, features = queries.shape
        heads = log_forget.shape[0]
        dh = features // heads
        share = heads // ring
        rows, columns = out_weight.shape

        def scans(kind):
            return [
                pltpu.VMEM((heads, dh, dh), kind),
                pltpu.VMEM((ring, share, dh, dh), kind),
                pltpu.VMEM((share, dh, dh), kind),
                pltpu.VMEM((share, dh, dh), kind),
                pltpu.VMEM((ring, share, dh, dh), kind),
                pltpu.VMEM((heads, dh, dh), kind),
            ]

        def pair(*shape):
            return [pltpu.SemaphoreType.DMA(shape), pltpu.SemaphoreType.DMA(shape)]

        vmem = pl.BlockSpec(memory_space=pltpu.VMEM)
        smem = pl.BlockSpec(memory_space=pltpu.SMEM)
        return pl.pallas_call(
            functools.partial(wrapped, functools.partial(kernel, layers, ring, heads)),
            out_shape=jax.ShapeDtypeStruct((tokens, columns), BF16),
            in_specs=[vmem, vmem, vmem, vmem, vmem, smem, vmem, vmem],
            out_specs=vmem,
            scratch_shapes=[
                pltpu.VMEM((ring, heads, dh), F32),
                *scans(BF16),
                *scans(F32),
                pltpu.VMEM((n * rows, columns), BF16),
                pltpu.VMEM((tokens, features), BF16),
                *pair(ring),
                *pair(2, ring),
                *pair(2, share),
                *pair(2, ring),
                *pair(layers),
                *pair(layers),
                *pair(layers * 2),
            ],
            compiler_params=pltpu.CompilerParams(
                collective_id=0, has_side_effects=True, vmem_limit_bytes=48 * 1024 * 1024),
        )(queries, keys, values, log_forget, input_gate, ridge, gain.reshape(1, features), out_weight)

    placed = (
        P(("parts", "seq"), None),
        P(("parts", "seq"), None),
        P(("parts", "seq"), None),
        P(None, ("parts", "seq")),
        P(None, ("parts", "seq")),
        P(),
        P(),
        P("seq", None),
    )
    return jax.shard_map(
        on_device, mesh=mesh, in_specs=placed, out_specs=P(("parts", "seq"), None), check_vma=False
    )
```

time: 204 us -> 72.2 us (0.35)
  the two profiles are of different devices: /device:TPU:0 before, /device:TPU:25 now
where the time goes in v1:
time: 72.2 us; the launch traced here: 71.9 us
  Pallas kernels  64.6 us (89%)
  local copies, waits for them, and re-layouts  7.31 us (10%)
    pallas_call x1, Pallas kernels, on_device(): pl.pallas_call(functools.partial(wrapped, functools.partial(kernel, layer...  64.6 us
    unnamed x17, local copies, waits for them, and re-layouts  7.31 us

profile of v1, /device:TPU:25, one launch (start us, length us, event | category | flops | bytes accessed | tf_op | source)
XLA Modules:
  0.0 71.9 jit_solution(5087234201468931847)
XLA Ops:
  0.0 0.0 copy-start.7
  0.0 0.7 copy-done.7
  0.7 0.0 copy-start
  0.7 0.9 %copy-done = bf16[128,1024]{1,0:T(8,128)(2,1)S(1)} copy-done((bf16[128,1024]{1,0:T(8,128)(2,1)S(1)}, bf16[128,1024]{1,0:T(8,128)(2,1)}, u32[]{:S(2)}) %copy-start) | copy-done | bytes 262168
  1.6 0.0 copy-start.1
  1.6 0.9 %copy-done.1 = bf16[128,1024]{1,0:T(8,128)(2,1)S(1)} copy-done((bf16[128,1024]{1,0:T(8,128)(2,1)S(1)}, bf16[128,1024]{1,0:T(8,128)(2,1)}, u32[]{:S(2)}) %copy-start.1) | copy-done | bytes 262168
  2.6 0.0 copy-start.2
  2.6 0.9 %copy-done.2 = bf16[128,1024]{1,0:T(8,128)(2,1)S(1)} copy-done((bf16[128,1024]{1,0:T(8,128)(2,1)S(1)}, bf16[128,1024]{1,0:T(8,128)(2,1)}, u32[]{:S(2)}) %copy-start.2) | copy-done | bytes 262168
  3.5 0.0 copy-start.3
  3.5 0.9 %copy-done.3 = bf16[64,2048]{1,0:T(8,128)(2,1)S(1)} copy-done((bf16[64,2048]{1,0:T(8,128)(2,1)S(1)}, bf16[64,2048]{1,0:T(8,128)(2,1)}, u32[]{:S(2)}) %copy-start.3) | copy-done | bytes 262168
  4.5 0.0 copy-start.4
  4.5 0.7 copy-done.4
  5.1 0.0 copy-start.5
  5.1 0.7 copy-done.5
  5.8 0.0 copy-start.6
  5.8 0.7 copy-done.6
  6.5 64.6 %shard_map.82 = bf16[128,2048]{1,0:T(8,128)(2,1)S(1)} custom-call(bf16[128,1024]{1,0:T(8,128)(2,1)S(1)} %copy-done, bf16[128,1024]{1,0:T(8,128)(2,1)S(1)} %copy-done.1, bf16[128,1024]{1,0:T(8,128)(2,1)S(1)} %copy-done.2, f32[8,128]{1,0:T(8,128)S(1)} %copy-done.4, f32[8,128]{1,0:T(8,128)S(1)} %copy-done.5, f32[8]{0:T(128)S(1)} %copy-done.7, ...), custom_call_target="tpu_custom_call" | custom-call | tf_op jit(solution)/shard_map/pallas_call | solution.py:314
  71.1 0.8 %copy.10 = bf16[128,2048]{1,0:T(8,128)(2,1)} copy(bf16[128,2048]{1,0:T(8,128)(2,1)S(1)} %shard_map.82) | data formatting | bytes 1048576
Async XLA Ops:
  0.0 0.7 copy-start.7
  0.7 0.9 %copy-start = (bf16[128,1024]{1,0:T(8,128)(2,1)S(1)}, bf16[128,1024]{1,0:T(8,128)(2,1)}, u32[]{:S(2)}) copy-start(bf16[128,1024]{1,0:T(8,128)(2,1)} %refs_0_.1) | copy-start | bytes 786436
  1.6 0.9 %copy-start.1 = (bf16[128,1024]{1,0:T(8,128)(2,1)S(1)}, bf16[128,1024]{1,0:T(8,128)(2,1)}, u32[]{:S(2)}) copy-start(bf16[128,1024]{1,0:T(8,128)(2,1)} %refs_1_.1) | copy-start | bytes 786436
  2.6 0.9 %copy-start.2 = (bf16[128,1024]{1,0:T(8,128)(2,1)S(1)}, bf16[128,1024]{1,0:T(8,128)(2,1)}, u32[]{:S(2)}) copy-start(bf16[128,1024]{1,0:T(8,128)(2,1)} %refs_2_.1) | copy-start | bytes 786436
  3.5 0.9 %copy-start.3 = (bf16[64,2048]{1,0:T(8,128)(2,1)S(1)}, bf16[64,2048]{1,0:T(8,128)(2,1)}, u32[]{:S(2)}) copy-start(bf16[64,2048]{1,0:T(8,128)(2,1)} %refs_7_.1) | copy-start | bytes 786436
  4.5 0.7 copy-start.4
  5.1 0.7 copy-start.5
  5.8 0.7 copy-start.6

commit v2 on v1

--- a/solution.py
+++ b/solution.py
@@ -30,27 +30,32 @@
 
 
 def kernel(
-    layers, ring, heads, q_ref, k_ref, v_ref, forget_ref, gate_ref, ridge_ref, gain_ref, w_ref,
-    out_ref, level, gram_out, gram_in, gram_chain_in, gram_chain_out, gram_back, gram_full,
+    layers, ring, heads, q_hbm, k_hbm, v_hbm, forget_hbm, gate_hbm, ridge_ref, gain_hbm, w_ref,
+    out_ref, q_ref, k_ref, v_ref, forget_ref, gate_ref, gain_ref, load_sems, level, gram_out, gram_in, gram_chain_in, gram_chain_out, gram_back, gram_full,
     state_out, state_in, state_chain_in, state_chain_out, state_back, state_full,
     weights, y_ref,
-    level_sems, piece_sems, chain_sems, back_sems, z_sems, y_sems, core_sems,
+    level_sems, piece_sems, chain_sems, back_sems, z_sems, y_sems, x_sems, core_sems,
 ):
     me = lax.axis_index("seq")
     layer, rank = me // ring, me % ring
     share = heads // ring
     tokens = q_ref.shape[0]
     dh = q_ref.shape[1] // heads
-    rows = w_ref.shape[0]
+    rows, columns = w_ref.shape
+    half = columns // 2
+    part = lax.axis_index("parts")
+    side = part % 2
+    twin = part + 1 - 2 * side
     pending = []
 
     def others():
         return [(rank + d) % ring for d in range(1, ring)]
 
-    def send(src, dst, sems, slot_out, slot_in, target):
+    def send(src, dst, sems, slot_out, slot_in, target, where=None):
         copy = pltpu.make_async_remote_copy(
             src_ref=src, dst_ref=dst, send_sem=sems[0].at[slot_out], recv_sem=sems[1].at[slot_in],
-            device_id={"seq": target}, device_id_type=MESH,
+            device_id={"seq": target} if where is None else {"parts": where, "seq": target},
+            device_id_type=MESH,
         )
         copy.start()
         return copy
@@ -61,15 +66,28 @@
             device_id={"seq": (me + 1) % (layers * ring)}, device_id_type=MESH,
         ).wait_recv()
 
-    def shard(index):
-        return weights.at[pl.ds(pl.multiple_of(index * rows, rows), rows)]
+    def piece_of(ref, index, part_side):
+        return ref.at[pl.ds(pl.multiple_of(index * rows, rows), rows),
+                      pl.ds(pl.multiple_of(part_side * half, 128), half)]
+
+    loads = []
+    for i, (src, dst) in enumerate((
+        (forget_hbm, forget_ref), (gate_hbm, gate_ref), (k_hbm, k_ref), (v_hbm, v_ref), (q_hbm, q_ref),
+        (gain_hbm, gain_ref), (w_ref, weights.at[pl.ds(pl.multiple_of(me * rows, rows), rows)]),
+    )):
+        loads.append(pltpu.make_async_copy(src, dst, load_sems.at[i]))
+        loads[-1].start()
 
     barrier = pltpu.get_barrier_semaphore()
     partners = [layer * ring + p for p in others()]
     partners += [((layer + d) % layers) * ring + rank for d in range(1, layers)]
     for partner in partners:
         pl.semaphore_signal(barrier, inc=1, device_id={"seq": partner}, device_id_type=MESH)
-    pl.semaphore_wait(barrier, len(partners))
+    pl.semaphore_signal(
+        barrier, inc=1, device_id={"parts": twin, "seq": me}, device_id_type=MESH)
+    pl.semaphore_wait(barrier, len(partners) + 1)
+    for load in loads[:4]:
+        load.wait()
 
     row_id = lax.broadcasted_iota(jnp.int32, (tokens, tokens), 0)
     col_id = lax.broadcasted_iota(jnp.int32, (tokens, tokens), 1)
@@ -87,26 +105,46 @@
 
     across = (rank + ring // 2) % ring
     sibling = rank + 1 - 2 * (rank % 2)
-    pending.append(send(w_ref, shard(me), y_sems, layer, layer, layer * ring + across))
-    pending.append(send(w_ref, shard(me), core_sems, layer * 2, layer * 2 + rank // 2, layer * ring + sibling))
-
-    def to_column():
-        for d in range(1, layers):
-            there = (layer + d) % layers
-            pending.append(send(w_ref, shard(me), z_sems, there, layer, there * ring + rank))
+    sibling_id = layer * ring + sibling
+
+    def to_sibling(index, part_side):
+        piece = piece_of(weights, index, part_side)
+        slot = index // ring * ring + index % ring // 2 * 2 + part_side
+        pending.append(send(piece, piece, core_sems, slot, slot, sibling_id))
+
+    def to_twin(index):
+        piece = piece_of(weights, index, side)
+        slot = index // ring * 2 + index % ring // 2
+        pending.append(send(piece, piece, x_sems, slot, slot, me, twin))
+
+    own = piece_of(w_ref, 0, side)
+    landing = piece_of(weights, me, side)
+    pending.append(send(own, landing, y_sems, layer, layer, layer * ring + across))
+    for d in range(1, layers):
+        there = (layer + d) % layers
+        pending.append(send(own, landing, z_sems, there, layer, there * ring + rank))
 
     def from_column(d):
         there = (layer + d) % layers
-        piece = shard(there * ring + rank)
+        index = there * ring + rank
+        piece = piece_of(weights, index, side)
         arrived(piece, z_sems, there)
         pending.append(send(piece, piece, y_sems, there, there, layer * ring + across))
-        pending.append(send(piece, piece, core_sems, there * 2, there * 2 + rank // 2, layer * ring + sibling))
+        to_twin(index)
+        to_sibling(index, side)
 
     def from_across(d):
         there = (layer + d) % layers
-        piece = shard(there * ring + across)
-        arrived(piece, y_sems, there)
-        pending.append(send(piece, piece, core_sems, there * 2 + 1, there * 2 + across // 2, layer * ring + sibling))
+        index = there * ring + across
+        arrived(piece_of(weights, index, side), y_sems, there)
+        to_twin(index)
+        to_sibling(index, side)
+
+    def from_twin(d, place):
+        there = (layer + d) % layers
+        index = there * ring + place
+        arrived(piece_of(weights, index, 1 - side), x_sems, there * 2 + place // 2)
+        to_sibling(index, 1 - side)
 
     pre, keys_t, keys_low, beta_keys = [], [], [], []
     mixes, decays = [], []
@@ -147,7 +185,9 @@
                 outgoing.at[pl.ds(p * share, share)], incoming.at[rank],
                 sems_of(piece_sems, kind), p, rank, layer * ring + p))
         incoming[rank] = outgoing[mine]
-    to_column()
+    loads[6].wait()
+    to_sibling(me, side)
+    to_sibling(me, 1 - side)
 
     for p in others():
         arrived(level.at[p], level_sems, p)
@@ -198,9 +238,9 @@
     scan(*kinds[1])
     for p in others():
         arrived(gram_full.at[pl.ds(p * share, share)], sems_of(back_sems, 0), p)
-    ahead = list(range(1, layers))
-    if ahead:
-        from_column(ahead.pop(0))
+    from_across(0)
+    for d in range(1, layers - 1):
+        from_column(d)
 
     starts = [gram_full[h] for h in range(heads)]
     systems, inverses, bounds = [], [], []
@@ -213,9 +253,10 @@
     for step in range(NEWTON - 1):
         rests = [low(2.0 * eye - dot(systems[h], inverses[h])) for h in range(heads)]
         inverses = [low(dot(inverses[h], rests[h])) for h in range(heads)]
-    from_across(0)
-    if ahead:
-        from_column(ahead.pop(0))
+    if layers > 1:
+        from_column(layers - 1)
+    loads[4].wait()
+    loads[5].wait()
 
     both = [jnp.concatenate([starts[h], keys_t[h]], axis=1) for h in range(heads)]
     queries, solved = [], []
@@ -224,7 +265,6 @@
         query = query * lax.rsqrt(jnp.sum(query * query, axis=1, keepdims=True) + EPS)
         queries.append(query)
         solved.append(dot(low(query), inverses[h]))
-    done = 1
     for step in range(CORR - 1):
         for h in range(heads):
             joint = dot(low(solved[h]), both[h])
@@ -234,14 +274,18 @@
                 + ridge_ref[h] * solved[h]
             )
             solved[h] = solved[h] + dot(low(queries[h] - applied), inverses[h])
-        while ahead and (step == CORR - 2 or len(ahead) > CORR - 2 - step):
-            from_column(ahead.pop(0))
-        if done < layers:
-            from_across(done)
-            done += 1
-    while done < layers:
-        from_across(done)
-        done += 1
+        if step == 0:
+            for d in range(1, layers - 1):
+                from_across(d)
+            for d in range(1, layers - 1):
+                from_twin(d, rank)
+        if step == 1:
+            if layers > 1:
+                from_across(layers - 1)
+                from_twin(layers - 1, rank)
+            from_twin(0, across)
+    for d in range(1, layers):
+        from_twin(d, across)
 
     for p in others():
         arrived(state_full.at[pl.ds(p * share, share)], sems_of(back_sems, 1), p)
@@ -255,12 +299,11 @@
         norm = lax.rsqrt(jnp.mean(output * output, axis=1, keepdims=True) + EPS)
         y_ref[:, lanes] = low(output * norm * gain_ref[:, lanes])
 
-    weights[pl.ds(pl.multiple_of(me * rows, rows), rows), :] = w_ref[...]
-    other = sibling
     for there in range(layers):
-        for half in range(ring // 2):
-            arrived(shard(there * ring + half * 2 + other % 2), core_sems, there * 2 + half)
-    columns = w_ref.shape[1]
+        for i in range(ring // 2):
+            for part_side in range(2):
+                index = there * ring + i * 2 + sibling % 2
+                arrived(piece_of(weights, index, part_side), core_sems, there * ring + i * 2 + part_side)
     width = min(512, columns)
     for c in range(0, columns, width):
         out_ref[:, c:c + width] = low(dot(y_ref[...], weights[:, c:c + width]))
@@ -279,9 +322,9 @@
 
 
 def wrapped(body, *refs):
-    tail = refs[-14:]
-    pairs = [(tail[i], tail[i + 1]) for i in range(0, 14, 2)]
-    body(*refs[:-14], *pairs)
+    tail = refs[-16:]
+    pairs = [(tail[i], tail[i + 1]) for i in range(0, 16, 2)]
+    body(*refs[:-16], *pairs)
 
 
 def solution(mesh):
@@ -310,13 +353,21 @@
             return [pltpu.SemaphoreType.DMA(shape), pltpu.SemaphoreType.DMA(shape)]
 
         vmem = pl.BlockSpec(memory_space=pltpu.VMEM)
+        hbm = pl.BlockSpec(memory_space=pltpu.HBM)
         smem = pl.BlockSpec(memory_space=pltpu.SMEM)
         return pl.pallas_call(
             functools.partial(wrapped, functools.partial(kernel, layers, ring, heads)),
             out_shape=jax.ShapeDtypeStruct((tokens, columns), BF16),
-            in_specs=[vmem, vmem, vmem, vmem, vmem, smem, vmem, vmem],
+            in_specs=[hbm, hbm, hbm, hbm, hbm, smem, hbm, hbm],
             out_specs=vmem,
             scratch_shapes=[
+                pltpu.VMEM((tokens, features), BF16),
+                pltpu.VMEM((tokens, features), BF16),
+                pltpu.VMEM((tokens, features), BF16),
+                pltpu.VMEM((heads, tokens), F32),
+                pltpu.VMEM((heads, tokens), F32),
+                pltpu.VMEM((1, features), F32),
+                pltpu.SemaphoreType.DMA((7,)),
                 pltpu.VMEM((ring, heads, dh), F32),
                 *scans(BF16),
                 *scans(F32),
@@ -329,9 +380,10 @@
                 *pair(layers),
                 *pair(layers),
                 *pair(layers * 2),
+                *pair(layers * ring),
             ],
             compiler_params=pltpu.CompilerParams(
-                collective_id=0, has_side_effects=True, vmem_limit_bytes=48 * 1024 * 1024),
+                collective_id=0, has_side_effects=True, vmem_limit_bytes=56 * 1024 * 1024),
         )(queries, keys, values, log_forget, input_gate, ridge, gain.reshape(1, features), out_weight)
 
     placed = (

time: 72.2 us -> 54.5 us (0.75)
  Pallas kernels: 64.6 us -> 52.5 us
  local copies, waits for them, and re-layouts: 7.31 us -> 1.88 us
    pallas_call x1, Pallas kernels: 64.6 us -> 52.5 us  [on_device(): pl.pallas_call(functools.partial(wrapped, functools.partial(kernel, layer...]
    unnamed x17 -> x1, local copies, waits for them, and re-layouts: 7.31 us -> 1.88 us
where the time goes in v2:
time: 54.5 us; the launch traced here: 54.4 us
  Pallas kernels  52.5 us (96%)
  local copies, waits for them, and re-layouts  1.88 us (3%)
    pallas_call x1, Pallas kernels, on_device(): pl.pallas_call(functools.partial(wrapped, functools.partial(kernel, layer...  52.5 us
    unnamed x1, local copies, waits for them, and re-layouts  1.88 us

profile of v2, /device:TPU:25, one launch (start us, length us, event | category | flops | bytes accessed | tf_op | source)
XLA Modules:
  0.0 54.4 jit_solution(17321703812469474281)
XLA Ops:
  0.0 52.5 %shard_map.82 = bf16[128,2048]{1,0:T(8,128)(2,1)} custom-call(bf16[128,1024]{1,0:T(8,128)(2,1)} %refs_0_.1, bf16[128,1024]{1,0:T(8,128)(2,1)} %refs_1_.1, bf16[128,1024]{1,0:T(8,128)(2,1)} %refs_2_.1, f32[8,128]{1,0:T(8,128)} %refs_3_.1, f32[8,128]{1,0:T(8,128)} %refs_4_.1, f32[8]{0:T(128)} %refs_5_.1, f32[1,1024]{1,0:T(1,128)} %bitcast.1, ...), custom_call_target="tpu_custom_call" | custom-call | tf_op jit(solution)/shard_map/pallas_call | solution.py:358
  52.5 1.9 %copy.10 = bf16[128,2048]{1,0:T(8,128)(2,1)} copy(bf16[128,2048]{1,0:T(8,128)(2,1)} %shard_map.82) | data formatting | bytes 1048576

commit v3 on v2

--- a/solution.py
+++ b/solution.py
@@ -22,11 +22,6 @@
 
 def low(a):
     return a.astype(BF16)
-
-
-def split_dot(a, b):
-    high = low(a)
-    return dot(high, b) + dot(low(a - high.astype(F32)), b)
 
 
 def kernel(
@@ -179,12 +174,15 @@
     def sems_of(sems, kind):
         return (sems[0].at[kind], sems[1].at[kind])
 
-    for outgoing, incoming, *_, kind in kinds:
+    def exchange(outgoing, incoming, *_):
+        kind = _[-1]
         for p in others():
             pending.append(send(
                 outgoing.at[pl.ds(p * share, share)], incoming.at[rank],
                 sems_of(piece_sems, kind), p, rank, layer * ring + p))
         incoming[rank] = outgoing[mine]
+
+    exchange(*kinds[0])
     loads[6].wait()
     to_sibling(me, side)
     to_sibling(me, 1 - side)
@@ -235,13 +233,9 @@
         chained.append((chain_out, chain_in, kind))
 
     scan(*kinds[0])
-    scan(*kinds[1])
+    exchange(*kinds[1])
     for p in others():
         arrived(gram_full.at[pl.ds(p * share, share)], sems_of(back_sems, 0), p)
-    from_across(0)
-    for d in range(1, layers - 1):
-        from_column(d)
-
     starts = [gram_full[h] for h in range(heads)]
     systems, inverses, bounds = [], [], []
     for h in range(heads):
@@ -253,6 +247,12 @@
     for step in range(NEWTON - 1):
         rests = [low(2.0 * eye - dot(systems[h], inverses[h])) for h in range(heads)]
         inverses = [low(dot(inverses[h], rests[h])) for h in range(heads)]
+        if step == 0:
+            from_across(0)
+            for d in range(1, layers - 1):
+                from_column(d)
+        if step == 2:
+            scan(*kinds[1])
     if layers > 1:
         from_column(layers - 1)
     loads[4].wait()
@@ -266,14 +266,13 @@
         queries.append(query)
         solved.append(dot(low(query), inverses[h]))
     for step in range(CORR - 1):
-        for h in range(heads):
-            joint = dot(low(solved[h]), both[h])
-            applied = (
-                decays[h] * joint[:, :dh]
-                + dot(low(mixes[h] * joint[:, dh:]), beta_keys[h])
-                + ridge_ref[h] * solved[h]
-            )
-            solved[h] = solved[h] + dot(low(queries[h] - applied), inverses[h])
+        joints = [dot(low(solved[h]), both[h]) for h in range(heads)]
+        mixed = [dot(low(mixes[h] * joints[h][:, dh:]), beta_keys[h]) for h in range(heads)]
+        rests = [
+            low(queries[h] - (decays[h] * joints[h][:, :dh] + mixed[h] + ridge_ref[h] * solved[h]))
+            for h in range(heads)
+        ]
+        solved = [solved[h] + dot(rests[h], inverses[h]) for h in range(heads)]
         if step == 0:
             for d in range(1, layers - 1):
                 from_across(d)
@@ -289,13 +288,19 @@
 
     for p in others():
         arrived(state_full.at[pl.ds(p * share, share)], sems_of(back_sems, 1), p)
+    joints, scores = [], []
+    for h in range(heads):
+        state = state_full[h]
+        near = low(state)
+        high = low(solved[h])
+        right = jnp.concatenate([near, keys_t[h]], axis=1)
+        joint = dot(high, right) + dot(low(solved[h] - high.astype(F32)), right)
+        joints.append(joint[:, :dh] + dot(high, low(state - near.astype(F32))))
+        scores.append(low(mixes[h] * joint[:, dh:]))
     for h in range(heads):
         lanes = slice(h * dh, (h + 1) * dh)
-        scores = mixes[h] * split_dot(solved[h], keys_t[h])
         value = low(gate_col[:, h:h + 1] * v_ref[:, lanes].astype(F32))
-        state = state_full[h]
-        output = decays[h] * split_dot(solved[h], low(state)) + dot(low(scores), value)
-        output = output + decays[h] * dot(low(solved[h]), low(state - low(state).astype(F32)))
+        output = decays[h] * joints[h] + dot(scores[h], value)
         norm = lax.rsqrt(jnp.mean(output * output, axis=1, keepdims=True) + EPS)
         y_ref[:, lanes] = low(output * norm * gain_ref[:, lanes])
 

time: 54.5 us -> 54.1 us (level)
  no operation moved by 1% of the time
where the time goes in v3:
time: 54.1 us; the launch traced here: 54 us
  Pallas kernels  52.1 us (96%)
  local copies, waits for them, and re-layouts  1.88 us (3%)
    pallas_call x1, Pallas kernels, on_device(): pl.pallas_call(functools.partial(wrapped, functools.partial(kernel, layer...  52.1 us
    unnamed x1, local copies, waits for them, and re-layouts  1.88 us

profile of v3, /device:TPU:25, one launch (start us, length us, event | category | flops | bytes accessed | tf_op | source)
XLA Modules:
  0.0 54.0 jit_solution(4945067674667389741)
XLA Ops:
  0.0 52.1 %shard_map.82 = bf16[128,2048]{1,0:T(8,128)(2,1)} custom-call(bf16[128,1024]{1,0:T(8,128)(2,1)} %refs_0_.1, bf16[128,1024]{1,0:T(8,128)(2,1)} %refs_1_.1, bf16[128,1024]{1,0:T(8,128)(2,1)} %refs_2_.1, f32[8,128]{1,0:T(8,128)} %refs_3_.1, f32[8,128]{1,0:T(8,128)} %refs_4_.1, f32[8]{0:T(128)} %refs_5_.1, f32[1,1024]{1,0:T(1,128)} %bitcast.1, ...), custom_call_target="tpu_custom_call" | custom-call | tf_op jit(solution)/shard_map/pallas_call | solution.py:363
  52.1 1.9 %copy.10 = bf16[128,2048]{1,0:T(8,128)(2,1)} copy(bf16[128,2048]{1,0:T(8,128)(2,1)} %shard_map.82) | data formatting | bytes 1048576

commit v4 on v3

--- a/solution.py
+++ b/solution.py
@@ -159,7 +159,7 @@
         made = dot(raw, right, ((0,), (0,)))
         gram_out[h] = low(made[:, :dh])
         pre.append(made[:, dh:2 * dh])
-        state_out[h] = made[:, 2 * dh:3 * dh]
+        state_out[h] = low(made[:, 2 * dh:3 * dh])
         keys_t.append(low(made[:, 3 * dh:]))
         beta_keys.append(low(beta * unit))
         mixes.append(jnp.where(lower, jnp.exp(jnp.minimum(run - run_row[h:h + 1, :], 0.0)), 0.0))
@@ -290,12 +290,11 @@
         arrived(state_full.at[pl.ds(p * share, share)], sems_of(back_sems, 1), p)
     joints, scores = [], []
     for h in range(heads):
-        state = state_full[h]
-        near = low(state)
+        near = state_full[h]
         high = low(solved[h])
         right = jnp.concatenate([near, keys_t[h]], axis=1)
         joint = dot(high, right) + dot(low(solved[h] - high.astype(F32)), right)
-        joints.append(joint[:, :dh] + dot(high, low(state - near.astype(F32))))
+        joints.append(joint[:, :dh])
         scores.append(low(mixes[h] * joint[:, dh:]))
     for h in range(heads):
         lanes = slice(h * dh, (h + 1) * dh)
@@ -375,7 +374,7 @@
                 pltpu.SemaphoreType.DMA((7,)),
                 pltpu.VMEM((ring, heads, dh), F32),
                 *scans(BF16),
-                *scans(F32),
+                *scans(BF16),
                 pltpu.VMEM((n * rows, columns), BF16),
                 pltpu.VMEM((tokens, features), BF16),
                 *pair(ring),

time: 54.1 us -> 53.2 us (0.983)
  Pallas kernels: 52.1 us -> 51.2 us
    pallas_call x1, Pallas kernels: 52.1 us -> 51.2 us  [on_device(): pl.pallas_call(functools.partial(wrapped, functools.partial(kernel, layer...]
where the time goes in v4:
time: 53.2 us; the launch traced here: 53 us
  Pallas kernels  51.2 us (96%)
  local copies, waits for them, and re-layouts  1.88 us (4%)
    pallas_call x1, Pallas kernels, on_device(): pl.pallas_call(functools.partial(wrapped, functools.partial(kernel, layer...  51.2 us
    unnamed x1, local copies, waits for them, and re-layouts  1.88 us

profile of v4, /device:TPU:25, one launch (start us, length us, event | category | flops | bytes accessed | tf_op | source)
XLA Modules:
  0.0 53.0 jit_solution(11074094224250027721)
XLA Ops:
  0.0 51.2 %shard_map.82 = bf16[128,2048]{1,0:T(8,128)(2,1)} custom-call(bf16[128,1024]{1,0:T(8,128)(2,1)} %refs_0_.1, bf16[128,1024]{1,0:T(8,128)(2,1)} %refs_1_.1, bf16[128,1024]{1,0:T(8,128)(2,1)} %refs_2_.1, f32[8,128]{1,0:T(8,128)} %refs_3_.1, f32[8,128]{1,0:T(8,128)} %refs_4_.1, f32[8]{0:T(128)} %refs_5_.1, f32[1,1024]{1,0:T(1,128)} %bitcast.1, ...), custom_call_target="tpu_custom_call" | custom-call | tf_op jit(solution)/shard_map/pallas_call | solution.py:362
  51.2 1.9 %copy.10 = bf16[128,2048]{1,0:T(8,128)(2,1)} copy(bf16[128,2048]{1,0:T(8,128)(2,1)} %shard_map.82) | data formatting | bytes 1048576
